TPU v7x, 256 devices: a whole 4x4x8 slice. The times are simulated.
256 devices in a mesh: row: 32 (over x, y, core), col: 8 (over z).
Axes of the slice: x: 4, y: 4, z: 8, core: 2. Of those that a mesh axis runs over, the one named last changes fastest.
Arguments:
- solution: float32 [64, 65536], P(None, ('row', 'col')), may hold values from -6 to 6
- residual: float32 [64, 262144], P(None, ('row', 'col')), may hold values from -6 to 6
- direction: float32 [64, 65536], P(None, ('row', 'col')), may hold values from -6 to 6
- jacobian_tiles: bfloat16 [2048, 40, 128, 128], P('row', 'col'), may hold values from -0.078125 to 0.078125
- tile_blocks: int32 [2048, 40], P('row', 'col'), may hold values from 0 to 63, as said below
- tile_counts: int32 [2048, 8], P('row', 'col'), may hold values from 1 to 5, as said below
Outputs:
- solution_next: float32 [64, 65536], P(None, ('row', 'col'))
- residual_next: float32 [64, 262144], P(None, ('row', 'col'))
- direction_next: float32 [64, 65536], P(None, ('row', 'col'))
Inputs may be any that keep to these rules, and one draw needn't show every extreme that they name: `tile_blocks`: within each sensor and parameter group the 5 entries are different. Only the first tile_counts[i, c] slots of sensor i in group c hold a tile; some sensor fills all 5 slots of every group.
All inputs are finite; a program needn't handle non-finite values.
Results may differ from a plain program's by a relative error of at most 0.023.
Values may be sent and summed in bfloat16 or wider, within the bound.
A program may use at most 128 MiB of HBM per device.

v0:
```python
import functools
import jax
import jax.numpy as jnp
from jax import lax
from jax.sharding import Mesh
from jax.sharding import PartitionSpec as P

CB_DEV = 64
ITERS = 2
ROW = ("row_0", "row_1", "row_2")
ROW_COL = ("row_0", "row_1", "row_2", "col")


def in_blocks(value, dim, devices):
    before, after = (value.shape[:dim], value.shape[dim + 1 :])
    return jnp.moveaxis(value.reshape(*before, devices, -1, *after), dim, 0)


def sent_and_summed(value, axis, dim):
    devices = lax.axis_size(axis)
    tiles = lax.all_to_all(in_blocks(value, dim, devices), axis, 0, 0, tiled=True)
    return jnp.sum(tiles.astype(jnp.float32), axis=0)


def over_axes(value, axes):
    return functools.reduce(lax.psum, axes, value)


def laid_out(tiles, dim):
    tiles = jnp.moveaxis(tiles, 0, dim)
    lengths = tiles.shape
    return tiles.reshape(*lengths[:dim], lengths[dim] * lengths[dim + 1], *lengths[dim + 2 :])


def copy_for_each(value, axis):
    devices = lax.axis_size(axis)
    return lax.all_to_all(
        jnp.broadcast_to(value[None], (devices, *value.shape)), axis, 0, 0, tiled=True
    )


def collect(value, axis, dim):
    return laid_out(copy_for_each(value, axis), dim)


def times_highest(left, right):
    return jnp.dot(left, right, precision=lax.Precision.HIGHEST)


def gram_matrix(values):
    return jnp.dot(values, values.T, precision=lax.Precision.HIGHEST)


def solve_spd(matrix, right):
    factor_low = jnp.linalg.cholesky(matrix)
    middle = lax.linalg.triangular_solve(factor_low, right, left_side=True, lower=True)
    return lax.linalg.triangular_solve(
        factor_low, middle, left_side=True, lower=True, transpose_a=True
    )


def images(jacobian_tiles, tile_blocks, live_slot, direction_half):
    rhs_count = direction_half.shape[0]
    tile_width = jacobian_tiles.shape[2]
    table_view = direction_half.reshape(rhs_count, -1, tile_width)
    picked = jnp.take(table_view, tile_blocks, axis=1) * live_slot[None, :, :, None]
    product = jnp.einsum(
        "rsab,nrsb->nra", jacobian_tiles, picked, preferred_element_type=jnp.float32
    )
    return product.reshape(rhs_count, -1)


def gradients(jacobian_tiles, tile_blocks, live_slot, rows_half):
    rhs_count = rows_half.shape[0]
    tile_width = jacobian_tiles.shape[2]
    sensors = jacobian_tiles.shape[0]
    row_view = rows_half.reshape(rhs_count, sensors, tile_width)
    contrib = jnp.einsum(
        "rsab,nra->rsnb", jacobian_tiles, row_view, preferred_element_type=jnp.float32
    )
    contrib = contrib * live_slot.astype(jnp.float32)[:, :, None, None]
    summed = jax.ops.segment_sum(
        contrib.reshape(-1, rhs_count, tile_width), tile_blocks.reshape(-1), num_segments=CB_DEV
    )
    return summed.transpose(1, 0, 2).reshape(rhs_count, CB_DEV * tile_width)


def per_device(solution, residual, direction, jacobian_tiles, tile_blocks, tile_counts):
    live_slot = (
        jnp.arange(jacobian_tiles.shape[1], dtype=jnp.int32)[None, :] < tile_counts
    ).astype(jnp.bfloat16)
    share_rows = residual.shape[1]
    col_start = lax.axis_index("col") * share_rows
    rows_now = lax.all_gather(residual.astype(jnp.bfloat16), "col", axis=1, tiled=True).astype(
        residual.dtype
    )

    def gradient_step(rows_value):
        rows_half = rows_value.astype(jnp.bfloat16)
        partial_term = gradients(jacobian_tiles, tile_blocks, live_slot, rows_half)
        gradient = sent_and_summed(partial_term.astype(jnp.bfloat16), ROW, 1)
        gamma_value = over_axes(gram_matrix(gradient), ROW_COL)
        return (gradient, gamma_value)

    gradient, gamma_now = gradient_step(rows_now)
    iterate = solution
    for iteration in range(ITERS):
        direction_half = collect(direction.astype(jnp.bfloat16), ROW, 1)
        image_partial_term = images(jacobian_tiles, tile_blocks, live_slot, direction_half)
        image = lax.psum(image_partial_term.astype(jnp.bfloat16), "col").astype(jnp.float32)
        curvature = over_axes(gram_matrix(image), ROW)
        image, curvature = (image, curvature)
        step_alpha = solve_spd(curvature, gamma_now)
        iterate = iterate + times_highest(step_alpha.T, direction)
        rows_now = rows_now - times_highest(step_alpha.T, image)
        gradient, gamma_next = gradient_step(rows_now)
        step_beta = solve_spd(gamma_now, gamma_next)
        direction = gradient + times_highest(step_beta.T, direction)
        gamma_now = gamma_next
    residual_out = lax.dynamic_slice_in_dim(rows_now, col_start, share_rows, 1)
    return (iterate, residual_out, direction)


def solution(mesh):
    torus = Mesh(
        mesh.devices.reshape(4, 4, 2, mesh.shape["col"]), ("row_0", "row_1", "row_2", "col")
    )
    in_specs = (
        P(None, ROW_COL),
        P(None, ROW_COL),
        P(None, ROW_COL),
        P(ROW, "col", None, None),
        P(ROW, "col"),
        P(ROW, "col"),
    )
    out_specs = (P(None, ROW_COL), P(None, ROW_COL), P(None, ROW_COL))
    return jax.shard_map(
        per_device, mesh=torus, in_specs=in_specs, out_specs=out_specs, check_vma=False
    )
```

profile of v0, /device:TPU:4, one launch (start us, length us, event | category | flops | bytes accessed | tf_op | source)
XLA Modules:
  0.0 678.9 jit_solution(5240777342642542572)
XLA Ops:
  9.1 7.6 %all-to-all-start = ((bf16[32,64,256]{2,1,0:T(8,128)(2,1)}), bf16[32,64,256]{2,1,0:T(8,128)(2,1)S(1)}, u32[]{:S(2)}, u32[]{:S(2)}) async-start(bf16[32,64,256]{2,1,0:T(8,128)(2,1)} %broadcast_in_dim.13), calls=%async_computation | async-start | bytes 2097152 | tf_op jit(solution)/shard_map/all_to_all | solution.py:37
  21.9 9.7 %all-to-all-done = bf16[32,64,256]{2,1,0:T(8,128)(2,1)S(1)} async-done(((bf16[32,64,256]{2,1,0:T(8,128)(2,1)}), bf16[32,64,256]{2,1,0:T(8,128)(2,1)S(1)}, u32[]{:S(2)}, u32[]{:S(2)}) %all-to-all-start) | async-done | bytes 1048608 | tf_op jit(solution)/shard_map/all_to_all | solution.py:37
  33.3 13.3 %gather_fusion = bf16[320,64,128]{2,1,0:T(8,128)(2,1)} fusion(bf16[64,64,128]{2,0,1:T(8,128)(2,1)S(1)} %copy.70, s32[1024]{0:T(1024)S(1)} %pad_clamp_fusion), kind=kCustom, calls=%fused_computation.clone | custom fusion | bytes 10487040 | tf_op jit(solution)/shard_map/jit(_take)/gather | solution.py:66
  46.6 10.1 %fusion.10 = bf16[64,8,8,128]{3,2,1,0:T(8,128)(2,1)S(1)} fusion(bf16[64,5,128,128]{3,2,1,0:T(8,128)(2,1)} %param.16, bf16[64,5,64,128]{3,2,1,0:T(8,128)(2,1)} %bitcast.164, pred[64,5]{1,0:T(8,128)(4,1)S(1)} %copy.67, bf16[64,5]{1,0:T(8,128)(2,1)S(1)} %get-tuple-element.13), kind=kOutput, calls=%fused_computation.27 | convolution fusion | flops 676855808 | bytes 16778176 | tf_op jit(solution)/shard_map/rsab,nrsb->nra/dot_general | solution.py:67
  62.9 10.2 %broadcast_multiply_fusion.2 = f32[64,64,5,128]{3,1,2,0:T(8,128)} fusion(f32[64,5]{1,0:T(8,128)S(1)} %get-tuple-element.14, bf16[64,5,128,128]{3,2,1,0:T(8,128)(2,1)} %param.16, bf16[64,64,128,1]{2,1,0,3:T(8,128)(2,1)S(1)} %bitcast.166), kind=kOutput, calls=%fused_computation.15 | convolution fusion | flops 673710080 | bytes 22021376 | tf_op jit(solution)/shard_map/rsab,nra->rsnb/dot_general | solution.py:78
  73.3 33.3 %scatter_fusion = f32[64,64,128]{2,1,0:T(8,128)S(1)} fusion(f32[64,64,128]{2,1,0:T(8,128)S(1)} %broadcast.78.clone, s32[320]{0:T(512)S(1)} %reshape.148, f32[320,64,128]{2,1,0:T(8,128)} %bitcast.161), kind=kCustom, calls=%fused_computation.2 | custom fusion | flops 2621440 | bytes 31458560 | tf_op jit(solution)/shard_map/scatter-add | solution.py:82
  109.5 7.4 %all-to-all-start.1 = ((bf16[32,64,256]{2,1,0:T(8,128)(2,1)}), bf16[32,64,256]{2,1,0:T(8,128)(2,1)S(1)}, u32[]{:S(2)}, u32[]{:S(2)}) async-start(bf16[32,64,256]{2,1,0:T(8,128)(2,1)} %copy.77), calls=%async_computation.1 | async-start | bytes 2097152 | tf_op jit(solution)/shard_map/all_to_all | solution.py:21
  116.9 21.1 %all-reduce.6.cloned.1.call-done = bf16[64,8192]{1,0:T(8,128)(2,1)} async-done(((bf16[64,8192]{1,0:T(8,128)(2,1)}), bf16[64,8192]{1,0:T(8,128)(2,1)}) %all-reduce.6.cloned.1.call-update) | async-done | bytes 1048592 | tf_op jit(solution)/shard_map/psum | solution.py:110
  140.3 16.0 %all-reduce.1 = (f32[64,64]{0,1:T(8,128)S(1)}, f32[64,64]{0,1:T(8,128)S(1)}) all-reduce(f32[64,64]{0,1:T(8,128)S(1)} %fusion.45, f32[64,64]{0,1:T(8,128)S(1)} %fusion.44), channel_id=1, replica_groups=mesh['row_0'=4,'row_1'=4,'row_2'=2,'col'=8] {'row_0'}, use_global_device_ids=true, to_apply=%region_8.0 | all-reduce | flops 8192 | bytes 65536 | tf_op jit(solution)/shard_map/psum | solution.py:26
  156.3 17.6 %all-reduce = (f32[64,64]{0,1:T(8,128)S(1)}, f32[64,64]{0,1:T(8,128)S(1)}) all-reduce(f32[64,64]{0,1:T(8,128)S(1)} %get-tuple-element.9, f32[64,64]{0,1:T(8,128)S(1)} %get-tuple-element.10), channel_id=1, replica_groups=mesh['row_0'=4,'row_1'=4,'row_2'=2,'col'=8] {'row_1'}, use_global_device_ids=true, to_apply=%region_9.0 | all-reduce | flops 8192 | bytes 65536 | tf_op jit(solution)/shard_map/psum | solution.py:26
  177.5 29.1 %psum.147 = f32[64,64]{0,1:T(8,128)S(1)} all-reduce(f32[64,64]{0,1:T(8,128)S(1)} %get-tuple-element.11), channel_id=1, replica_groups=mesh['row_0'=4,'row_1'=4,'row_2'=2,'col'=8] {'col'}, use_global_device_ids=true, to_apply=%region_11.14 | all-reduce | flops 4096 | bytes 32768 | tf_op jit(solution)/shard_map/psum | solution.py:26
  206.7 5.8 cholesky.74
  223.3 10.2 %broadcast_multiply_fusion.1 = f32[64,64,5,128]{3,1,2,0:T(8,128)} fusion(f32[64,5]{1,0:T(8,128)S(1)} %get-tuple-element.14, bf16[64,5,128,128]{3,2,1,0:T(8,128)(2,1)} %param.16, bf16[64,64,128,1]{2,1,0,3:T(8,128)(2,1)S(1)} %bitcast.167), kind=kOutput, calls=%fused_computation.14 | convolution fusion | flops 673710080 | bytes 22021376 | tf_op jit(solution)/shard_map/rsab,nra->rsnb/dot_general | solution.py:78
  233.7 33.0 %scatter_fusion.1 = f32[64,64,128]{2,1,0:T(8,128)S(1)} fusion(f32[64,64,128]{2,1,0:T(8,128)S(1)} %broadcast.78.clone.1, s32[320]{0:T(512)S(1)} %reshape.148, f32[320,64,128]{2,1,0:T(8,128)} %bitcast.162), kind=kCustom, calls=%fused_computation.3 | custom fusion | flops 2621440 | bytes 31458560 | tf_op jit(solution)/shard_map/scatter-add | solution.py:82
  269.6 16.1 %all-to-all-start.2 = ((bf16[32,64,256]{2,1,0:T(8,128)(2,1)}), bf16[32,64,256]{2,1,0:T(8,128)(2,1)S(1)}, u32[]{:S(2)}, u32[]{:S(2)}) async-start(bf16[32,64,256]{2,1,0:T(8,128)(2,1)} %copy.82), calls=%async_computation.2 | async-start | bytes 2097152 | tf_op jit(solution)/shard_map/all_to_all | solution.py:21
  285.8 5.8 cholesky.85
  300.8 16.0 %psum.148 = f32[64,64]{0,1:T(8,128)S(1)} all-reduce(f32[64,64]{0,1:T(8,128)S(1)} %fusion.46), channel_id=1, replica_groups=mesh['row_0'=4,'row_1'=4,'row_2'=2,'col'=8] {'row_0'}, use_global_device_ids=true, to_apply=%region_14.19 | all-reduce | flops 4096 | bytes 32768 | tf_op jit(solution)/shard_map/psum | solution.py:26
  316.8 15.4 %psum.149 = f32[64,64]{0,1:T(8,128)S(1)} all-reduce(f32[64,64]{0,1:T(8,128)S(1)} %psum.148), channel_id=1, replica_groups=mesh['row_0'=4,'row_1'=4,'row_2'=2,'col'=8] {'row_1'}, use_global_device_ids=true, to_apply=%region_15.20 | all-reduce | flops 4096 | bytes 32768 | tf_op jit(solution)/shard_map/psum | solution.py:26
  335.7 27.1 %psum.151 = f32[64,64]{0,1:T(8,128)S(1)} all-reduce(f32[64,64]{0,1:T(8,128)S(1)} %psum.150), channel_id=1, replica_groups=mesh['row_0'=4,'row_1'=4,'row_2'=2,'col'=8] {'col'}, use_global_device_ids=true, to_apply=%region_17.22 | all-reduce | flops 4096 | bytes 32768 | tf_op jit(solution)/shard_map/psum | solution.py:26
  363.5 20.5 %all_to_all.25 = bf16[32,64,256]{2,1,0:T(8,128)(2,1)S(1)} all-to-all(bf16[32,64,256]{2,1,0:T(8,128)(2,1)S(1)} %broadcast_in_dim.15), channel_id=1, replica_groups=mesh['row_0'=4,'row_1'=4,'row_2'=2,'col'=8] {'row_0','row_1','row_2'}, dimensions={0} | all-to-all | bytes 2097152 | tf_op jit(solution)/shard_map/all_to_all | solution.py:37
  385.7 13.3 %gather_fusion.1 = bf16[320,64,128]{2,1,0:T(8,128)(2,1)} fusion(bf16[64,64,128]{2,0,1:T(8,128)(2,1)S(1)} %copy.87, s32[1024]{0:T(1024)S(1)} %pad_clamp_fusion), kind=kCustom, calls=%fused_computation.1.clone | custom fusion | bytes 10487040 | tf_op jit(solution)/shard_map/jit(_take)/gather | solution.py:66
  399.1 10.0 %fusion.11 = bf16[64,8,8,128]{3,2,1,0:T(8,128)(2,1)S(1)} fusion(bf16[64,5,128,128]{3,2,1,0:T(8,128)(2,1)} %param.16, bf16[64,5,64,128]{3,2,1,0:T(8,128)(2,1)} %bitcast.163, pred[64,5]{1,0:T(8,128)(4,1)S(1)} %copy.67, bf16[64,5]{1,0:T(8,128)(2,1)S(1)} %get-tuple-element.13), kind=kOutput, calls=%fused_computation.28 | convolution fusion | flops 676855808 | bytes 16778176 | tf_op jit(solution)/shard_map/rsab,nrsb->nra/dot_general | solution.py:67
  410.7 72.9 %all-reduce.8.cloned.1.call-done = bf16[64,8192]{1,0:T(8,128)(2,1)} async-done(((bf16[64,8192]{1,0:T(8,128)(2,1)}), bf16[64,8192]{1,0:T(8,128)(2,1)}) %all-reduce.8.cloned.1.call-update) | async-done | bytes 1048592 | tf_op jit(solution)/shard_map/psum | solution.py:110
  485.6 15.5 %psum.153 = f32[64,64]{0,1:T(8,128)S(1)} all-reduce(f32[64,64]{0,1:T(8,128)S(1)} %fusion.47), channel_id=1, replica_groups=mesh['row_0'=4,'row_1'=4,'row_2'=2,'col'=8] {'row_0'}, use_global_device_ids=true, to_apply=%region_19.24 | all-reduce | flops 4096 | bytes 32768 | tf_op jit(solution)/shard_map/psum | solution.py:26
  501.1 17.0 %psum.154 = f32[64,64]{0,1:T(8,128)S(1)} all-reduce(f32[64,64]{0,1:T(8,128)S(1)} %psum.153), channel_id=1, replica_groups=mesh['row_0'=4,'row_1'=4,'row_2'=2,'col'=8] {'row_1'}, use_global_device_ids=true, to_apply=%region_20.25 | all-reduce | flops 4096 | bytes 32768 | tf_op jit(solution)/shard_map/psum | solution.py:26
  521.9 5.8 cholesky.96
  538.5 10.2 %broadcast_multiply_fusion = f32[64,64,5,128]{3,1,2,0:T(8,128)} fusion(f32[64,5]{1,0:T(8,128)S(1)} %get-tuple-element.14, bf16[64,5,128,128]{3,2,1,0:T(8,128)(2,1)} %param.16, bf16[64,64,128,1]{2,1,0,3:T(8,128)(2,1)S(1)} %bitcast.165), kind=kOutput, calls=%fused_computation.13 | convolution fusion | flops 673710080 | bytes 22021376 | tf_op jit(solution)/shard_map/rsab,nra->rsnb/dot_general | solution.py:78
  548.9 33.0 %scatter_fusion.2 = f32[64,64,128]{2,1,0:T(8,128)S(1)} fusion(f32[64,64,128]{2,1,0:T(8,128)S(1)} %broadcast.78, s32[320]{0:T(512)S(1)} %reshape.148, f32[320,64,128]{2,1,0:T(8,128)} %bitcast.160), kind=kCustom, calls=%fused_computation.4 | custom fusion | flops 2621440 | bytes 31458560 | tf_op jit(solution)/shard_map/scatter-add | solution.py:82
  590.6 5.8 cholesky.107
  605.8 15.9 %psum.156 = f32[64,64]{1,0:T(8,128)S(1)} all-reduce(f32[64,64]{1,0:T(8,128)S(1)} %fusion.48), channel_id=1, replica_groups=mesh['row_0'=4,'row_1'=4,'row_2'=2,'col'=8] {'row_0'}, use_global_device_ids=true, to_apply=%region_24.29 | all-reduce | flops 4096 | bytes 32768 | tf_op jit(solution)/shard_map/psum | solution.py:26
  621.7 16.4 %psum.157 = f32[64,64]{1,0:T(8,128)S(1)} all-reduce(f32[64,64]{1,0:T(8,128)S(1)} %psum.156), channel_id=1, replica_groups=mesh['row_0'=4,'row_1'=4,'row_2'=2,'col'=8] {'row_1'}, use_global_device_ids=true, to_apply=%region_25.30 | all-reduce | flops 4096 | bytes 32768 | tf_op jit(solution)/shard_map/psum | solution.py:26
  641.6 29.1 %psum.159 = f32[64,64]{1,0:T(8,128)S(1)} all-reduce(f32[64,64]{1,0:T(8,128)S(1)} %psum.158), channel_id=1, replica_groups=mesh['row_0'=4,'row_1'=4,'row_2'=2,'col'=8] {'col'}, use_global_device_ids=true, to_apply=%region_27.32 | all-reduce | flops 4096 | bytes 32768 | tf_op jit(solution)/shard_map/psum | solution.py:26
  (115 shorter events, 93.7 us)
Async XLA Ops:
  9.1 22.5 %all-to-all-start = ((bf16[32,64,256]{2,1,0:T(8,128)(2,1)}), bf16[32,64,256]{2,1,0:T(8,128)(2,1)S(1)}, u32[]{:S(2)}, u32[]{:S(2)}) async-start(bf16[32,64,256]{2,1,0:T(8,128)(2,1)} %broadcast_in_dim.13), calls=%async_computation | async-start | bytes 2097152 | tf_op jit(solution)/shard_map/all_to_all | solution.py:37
  16.7 44.7 %all-gather.2.cloned.1.call-start = ((), (), s32[]{:S(2)}) async-start(), calls=%async_computation.6 | async-start | bytes 1179648 | tf_op jit(solution)/shard_map/all_gather | solution.py:94
  18.4 119.6 %all-reduce.6.cloned.1.call-start = ((), (), s32[]{:S(2)}) async-start(), calls=%async_computation.5 | async-start | bytes 2097152 | tf_op jit(solution)/shard_map/psum | solution.py:110
  107.5 111.7 %copy-start.3 = (bf16[64,8192]{1,0:T(8,128)(2,1)S(1)}, bf16[64,8192]{1,0:T(8,128)(2,1)}, u32[]{:S(2)}) copy-start(bf16[64,8192]{1,0:T(8,128)(2,1)} %all-gather.2.cloned.1.call-done) | copy-start | bytes 3145732
  109.5 30.5 %all-to-all-start.1 = ((bf16[32,64,256]{2,1,0:T(8,128)(2,1)}), bf16[32,64,256]{2,1,0:T(8,128)(2,1)S(1)}, u32[]{:S(2)}, u32[]{:S(2)}) async-start(bf16[32,64,256]{2,1,0:T(8,128)(2,1)} %copy.77), calls=%async_computation.1 | async-start | bytes 2097152 | tf_op jit(solution)/shard_map/all_to_all | solution.py:21
  221.6 1.3 copy-start
  266.9 96.3 %copy-start.4 = (f32[64,256]{1,0:T(8,128)S(1)}, f32[64,256]{1,0:T(8,128)}, u32[]{:S(2)}) copy-start(f32[64,256]{1,0:T(8,128)} %param.15) | copy-start | bytes 196612
  269.6 30.8 %all-to-all-start.2 = ((bf16[32,64,256]{2,1,0:T(8,128)(2,1)}), bf16[32,64,256]{2,1,0:T(8,128)(2,1)S(1)}, u32[]{:S(2)}, u32[]{:S(2)}) async-start(bf16[32,64,256]{2,1,0:T(8,128)(2,1)} %copy.82), calls=%async_computation.2 | async-start | bytes 2097152 | tf_op jit(solution)/shard_map/all_to_all | solution.py:21
  285.7 198.0 %all-reduce.8.cloned.1.call-start = ((), (), s32[]{:S(2)}) async-start(), calls=%async_computation.7 | async-start | bytes 2097152 | tf_op jit(solution)/shard_map/psum | solution.py:110
  399.1 11.3 %copy-start.5 = (f32[64,256]{1,0:T(8,128)S(1)}, f32[64,256]{1,0:T(8,128)}, u32[]{:S(2)}) copy-start(f32[64,256]{1,0:T(8,128)} %param.13) | copy-start | bytes 196612
  409.1 125.3 %copy-start.1 = (f32[64,8192]{1,0:T(8,128)S(1)}, f32[64,8192]{1,0:T(8,128)}, u32[]{:S(2)}) copy-start(f32[64,8192]{1,0:T(8,128)} %copy-done) | copy-start | bytes 6291460
  536.7 1.3 copy-start.2
  584.7 20.7 %all-to-all-start.4 = ((bf16[32,64,256]{2,1,0:T(8,128)(2,1)}), bf16[32,64,256]{2,1,0:T(8,128)(2,1)S(1)}, u32[]{:S(2)}, u32[]{:S(2)}) async-start(bf16[32,64,256]{2,1,0:T(8,128)(2,1)} %copy.93), calls=%async_computation.4 | async-start | bytes 2097152 | tf_op jit(solution)/shard_map/all_to_all | solution.py:21
Sparse Core Ops, SparseCore 0:
  19.9 41.4 all-gather.1
  63.8 74.1 all-reduce.5
  410.5 73.1 all-reduce.7
where the time goes:
time: 692 us; the launch traced here: 679 us
  blocking collectives  250 us (36%)
  other arithmetic  154 us (22%)
  waiting for transfers between devices  110 us (16%)
  matrix products  63.6 us (9%)
  local copies, waits for them, and re-layouts  50.2 us (7%)
  starting transfers between devices  37 us (5%)
  between operations  14.8 us (2%)
    psum x15, blocking collectives, over_axes(): return functools.reduce(lax.psum, axes, value)  229 us
    scatter-add x3, other arithmetic, gradients(): jax.ops.segment_sum(contrib.reshape(-1, rhs_count, tile_width), tile_bloc...  99.3 us
    psum x2, waiting for transfers between devices, per_device(): lax.psum(image_partial_term.astype(jnp.bfloat16), 'col').astype(jnp.float32)  94 us
    dot_general x3, matrix products, gradients(): jnp.einsum('rsab,nra->rsnb', jacobian_tiles, row_view, preferred_element_...  30.5 us
    all_to_all x3, starting transfers between devices, sent_and_summed(): lax.all_to_all(in_blocks(value, dim, devices), axis, 0, 0, tiled=True)  29.3 us
    gather x2, local copies, waits for them, and re-layouts, images(): jnp.take(table_view, tile_blocks, axis=1) * live_slot[None, :, :, None]  26.7 us
    another operation x12, other arithmetic, solve_spd(): factor_low = jnp.linalg.cholesky(matrix)  26.1 us
    another operation x8, other arithmetic, solve_spd(): lax.linalg.triangular_solve(factor_low, middle, left_side=True, lower=Tru...  22.2 us
  transfers between devices with their start and end apart: 7, of which 6 were waited for; matrix products, arithmetic and copies ran while one was open for 16% of the time, Pallas kernels for 0%

commit v1 on v0

--- a/solution.py
+++ b/solution.py
@@ -9,6 +9,11 @@
 ITERS = 2
 ROW = ("row_0", "row_1", "row_2")
 ROW_COL = ("row_0", "row_1", "row_2", "col")
+
+
+def balance_trees(m, dev_axis):
+    q_next = lax.all_gather(m, dev_axis)
+    return jnp.sum(q_next, axis=0)
 
 
 def in_blocks(value, dim, devices):
@@ -107,7 +112,7 @@
     for iteration in range(ITERS):
         direction_half = collect(direction.astype(jnp.bfloat16), ROW, 1)
         image_partial_term = images(jacobian_tiles, tile_blocks, live_slot, direction_half)
-        image = lax.psum(image_partial_term.astype(jnp.bfloat16), "col").astype(jnp.float32)
+        image = balance_trees(image_partial_term.astype(jnp.bfloat16), "col").astype(jnp.float32)
         curvature = over_axes(gram_matrix(image), ROW)
         image, curvature = (image, curvature)
         step_alpha = solve_spd(curvature, gamma_now)

time: 692 us -> 723 us (1.045)
  waiting for transfers between devices: 110 us -> 133 us
  blocking collectives: 250 us -> 270 us
  starting transfers between devices: 37 us -> 19.4 us
  other arithmetic: 154 us -> 163 us
    all_gather x0 -> x2, waiting for transfers between devices: none -> 117 us  [balance_trees(): q_next = lax.all_gather(m, dev_axis)]
    psum x2 -> x0, waiting for transfers between devices: 94 us -> none  [per_device(): lax.psum(image_partial_term.astype(jnp.bfloat16), 'col').astype(jnp.float32)]
    all_to_all x0 -> x1, blocking collectives: none -> 22.1 us  [sent_and_summed(): lax.all_to_all(in_blocks(value, dim, devices), axis, 0, 0, tiled=True)]
    all_to_all x3 -> x2, starting transfers between devices: 29.3 us -> 11.7 us  [sent_and_summed(): lax.all_to_all(in_blocks(value, dim, devices), axis, 0, 0, tiled=True)]
    reduce_sum x0 -> x2, other arithmetic: none -> 9.9 us  [balance_trees(): return jnp.sum(q_next, axis=0)]
  transfers between devices with their start and end apart: 7 -> 6, of which waited for: 6 -> 6; matrix products, arithmetic and copies ran while one was open for 16% -> 15% of each run, Pallas kernels for 0% -> 0%
where the time goes in v1:
time: 723 us; the launch traced here: 709 us
  blocking collectives  270 us (37%)
  other arithmetic  163 us (23%)
  waiting for transfers between devices  133 us (18%)
  matrix products  58.1 us (8%)
  local copies, waits for them, and re-layouts  50.1 us (7%)
  starting transfers between devices  19.4 us (3%)
  between operations  14.8 us (2%)
    psum x15, blocking collectives, over_axes(): return functools.reduce(lax.psum, axes, value)  228 us
    all_gather x2, waiting for transfers between devices, balance_trees(): q_next = lax.all_gather(m, dev_axis)  117 us
    scatter-add x3, other arithmetic, gradients(): jax.ops.segment_sum(contrib.reshape(-1, rhs_count, tile_width), tile_bloc...  99.1 us
    dot_general x3, matrix products, gradients(): jnp.einsum('rsab,nra->rsnb', jacobian_tiles, row_view, preferred_element_...  30.5 us
    gather x2, local copies, waits for them, and re-layouts, images(): jnp.take(table_view, tile_blocks, axis=1) * live_slot[None, :, :, None]  26.7 us
    another operation x12, other arithmetic, solve_spd(): factor_low = jnp.linalg.cholesky(matrix)  26.1 us
    another operation x8, other arithmetic, solve_spd(): lax.linalg.triangular_solve(factor_low, middle, left_side=True, lower=Tru...  22.2 us
    all_to_all x1, blocking collectives, sent_and_summed(): lax.all_to_all(in_blocks(value, dim, devices), axis, 0, 0, tiled=True)  22.1 us
  transfers between devices with their start and end apart: 6, of which 6 were waited for; matrix products, arithmetic and copies ran while one was open for 15% of the time, Pallas kernels for 0%

profile of v1, /device:TPU:4, one launch (start us, length us, event | category | flops | bytes accessed | tf_op | source)
XLA Modules:
  0.0 709.3 jit_solution(13776926576667168792)
XLA Ops:
  9.1 7.6 %all-to-all-start = ((bf16[32,64,256]{2,1,0:T(8,128)(2,1)}), bf16[32,64,256]{2,1,0:T(8,128)(2,1)S(1)}, u32[]{:S(2)}, u32[]{:S(2)}) async-start(bf16[32,64,256]{2,1,0:T(8,128)(2,1)} %broadcast_in_dim.13), calls=%async_computation | async-start | bytes 2097152 | tf_op jit(solution)/shard_map/all_to_all | solution.py:42
  21.0 10.6 %all-to-all-done = bf16[32,64,256]{2,1,0:T(8,128)(2,1)S(1)} async-done(((bf16[32,64,256]{2,1,0:T(8,128)(2,1)}), bf16[32,64,256]{2,1,0:T(8,128)(2,1)S(1)}, u32[]{:S(2)}, u32[]{:S(2)}) %all-to-all-start) | async-done | bytes 1048608 | tf_op jit(solution)/shard_map/all_to_all | solution.py:42
  33.3 13.3 %gather_fusion = bf16[320,64,128]{2,1,0:T(8,128)(2,1)} fusion(bf16[64,64,128]{2,0,1:T(8,128)(2,1)S(1)} %copy.70, s32[1024]{0:T(1024)S(1)} %pad_clamp_fusion), kind=kCustom, calls=%fused_computation.clone | custom fusion | bytes 10487040 | tf_op jit(solution)/shard_map/jit(_take)/gather | solution.py:71
  46.6 10.1 %fusion.10 = bf16[64,64,128]{2,0,1:T(8,128)(2,1)S(1)} fusion(bf16[64,5,128,128]{3,2,1,0:T(8,128)(2,1)} %param.16, bf16[64,5,64,128]{3,2,1,0:T(8,128)(2,1)} %bitcast.156, pred[64,5]{1,0:T(8,128)(4,1)S(1)} %copy.67, bf16[64,5]{1,0:T(8,128)(2,1)S(1)} %get-tuple-element.13), kind=kOutput, calls=%fused_computation.27 | convolution fusion | flops 676855808 | bytes 16778176 | tf_op jit(solution)/shard_map/rsab,nrsb->nra/dot_general | solution.py:72
  62.9 10.2 %broadcast_multiply_fusion.2 = f32[64,64,5,128]{3,1,2,0:T(8,128)} fusion(f32[64,5]{1,0:T(8,128)S(1)} %get-tuple-element.14, bf16[64,5,128,128]{3,2,1,0:T(8,128)(2,1)} %param.16, bf16[64,64,128,1]{2,1,0,3:T(8,128)(2,1)S(1)} %bitcast.158), kind=kOutput, calls=%fused_computation.15 | convolution fusion | flops 673710080 | bytes 22021376 | tf_op jit(solution)/shard_map/rsab,nra->rsnb/dot_general | solution.py:83
  73.3 33.1 %scatter_fusion = f32[64,64,128]{2,1,0:T(8,128)S(1)} fusion(f32[64,64,128]{2,1,0:T(8,128)S(1)} %broadcast.78.clone, s32[320]{0:T(512)S(1)} %reshape.168, f32[320,64,128]{2,1,0:T(8,128)} %bitcast.153), kind=kCustom, calls=%fused_computation.2 | custom fusion | flops 2621440 | bytes 31458560 | tf_op jit(solution)/shard_map/scatter-add | solution.py:87
  108.3 22.1 %all_to_all.25 = bf16[32,64,256]{2,1,0:T(8,128)(2,1)S(1)} all-to-all(bf16[32,64,256]{2,1,0:T(8,128)(2,1)S(1)} %copy.77), channel_id=1, replica_groups=mesh['row_0'=4,'row_1'=4,'row_2'=2,'col'=8] {'row_0','row_1','row_2'}, dimensions={0} | all-to-all | bytes 2097152 | tf_op jit(solution)/shard_map/all_to_all | solution.py:26
  130.7 25.0 %all-gather.4.cloned.1.call-done = bf16[8,64,8192]{2,1,0:T(8,128)(2,1)} async-done(((bf16[1,64,8192]{2,1,0:T(8,128)(2,1)}), bf16[8,64,8192]{2,1,0:T(8,128)(2,1)}) %all-gather.4.cloned.1.call-update) | async-done | bytes 8388624 | tf_op jit(solution)/shard_map/all_gather | solution.py:15
  161.1 16.0 %all-reduce.1 = (f32[64,64]{0,1:T(8,128)S(1)}, f32[64,64]{0,1:T(8,128)S(1)}) all-reduce(f32[64,64]{0,1:T(8,128)S(1)} %fusion.45, f32[64,64]{0,1:T(8,128)S(1)} %fusion.44), channel_id=1, replica_groups=mesh['row_0'=4,'row_1'=4,'row_2'=2,'col'=8] {'row_0'}, use_global_device_ids=true, to_apply=%region_8.0 | all-reduce | flops 8192 | bytes 65536 | tf_op jit(solution)/shard_map/psum | solution.py:31
  177.0 17.7 %all-reduce = (f32[64,64]{0,1:T(8,128)S(1)}, f32[64,64]{0,1:T(8,128)S(1)}) all-reduce(f32[64,64]{0,1:T(8,128)S(1)} %get-tuple-element.9, f32[64,64]{0,1:T(8,128)S(1)} %get-tuple-element.10), channel_id=1, replica_groups=mesh['row_0'=4,'row_1'=4,'row_2'=2,'col'=8] {'row_1'}, use_global_device_ids=true, to_apply=%region_9.0 | all-reduce | flops 8192 | bytes 65536 | tf_op jit(solution)/shard_map/psum | solution.py:31
  198.3 28.3 %psum.132 = f32[64,64]{0,1:T(8,128)S(1)} all-reduce(f32[64,64]{0,1:T(8,128)S(1)} %get-tuple-element.11), channel_id=1, replica_groups=mesh['row_0'=4,'row_1'=4,'row_2'=2,'col'=8] {'col'}, use_global_device_ids=true, to_apply=%region_11.14 | all-reduce | flops 4096 | bytes 32768 | tf_op jit(solution)/shard_map/psum | solution.py:31
  226.7 5.8 cholesky.74
  242.1 10.2 %broadcast_multiply_fusion.1 = f32[64,64,5,128]{3,1,2,0:T(8,128)} fusion(f32[64,5]{1,0:T(8,128)S(1)} %get-tuple-element.14, bf16[64,5,128,128]{3,2,1,0:T(8,128)(2,1)} %param.16, bf16[64,64,128,1]{2,1,0,3:T(8,128)(2,1)S(1)} %bitcast.159), kind=kOutput, calls=%fused_computation.14 | convolution fusion | flops 673710080 | bytes 22021376 | tf_op jit(solution)/shard_map/rsab,nra->rsnb/dot_general | solution.py:83
  252.5 33.0 %scatter_fusion.1 = f32[64,64,128]{2,1,0:T(8,128)S(1)} fusion(f32[64,64,128]{2,1,0:T(8,128)S(1)} %broadcast.78.clone.1, s32[320]{0:T(512)S(1)} %reshape.168, f32[320,64,128]{2,1,0:T(8,128)} %bitcast.154), kind=kCustom, calls=%fused_computation.3 | custom fusion | flops 2621440 | bytes 31458560 | tf_op jit(solution)/shard_map/scatter-add | solution.py:87
  288.4 5.9 all-to-all-start.2
  294.4 5.8 cholesky.85
  309.4 15.9 %psum.133 = f32[64,64]{0,1:T(8,128)S(1)} all-reduce(f32[64,64]{0,1:T(8,128)S(1)} %fusion.46), channel_id=1, replica_groups=mesh['row_0'=4,'row_1'=4,'row_2'=2,'col'=8] {'row_0'}, use_global_device_ids=true, to_apply=%region_14.19 | all-reduce | flops 4096 | bytes 32768 | tf_op jit(solution)/shard_map/psum | solution.py:31
  325.4 15.5 %psum.134 = f32[64,64]{0,1:T(8,128)S(1)} all-reduce(f32[64,64]{0,1:T(8,128)S(1)} %psum.133), channel_id=1, replica_groups=mesh['row_0'=4,'row_1'=4,'row_2'=2,'col'=8] {'row_1'}, use_global_device_ids=true, to_apply=%region_15.20 | all-reduce | flops 4096 | bytes 32768 | tf_op jit(solution)/shard_map/psum | solution.py:31
  344.3 27.1 %psum.136 = f32[64,64]{0,1:T(8,128)S(1)} all-reduce(f32[64,64]{0,1:T(8,128)S(1)} %psum.135), channel_id=1, replica_groups=mesh['row_0'=4,'row_1'=4,'row_2'=2,'col'=8] {'col'}, use_global_device_ids=true, to_apply=%region_17.22 | all-reduce | flops 4096 | bytes 32768 | tf_op jit(solution)/shard_map/psum | solution.py:31
  372.1 20.7 %all_to_all.26 = bf16[32,64,256]{2,1,0:T(8,128)(2,1)S(1)} all-to-all(bf16[32,64,256]{2,1,0:T(8,128)(2,1)S(1)} %broadcast_in_dim.15), channel_id=1, replica_groups=mesh['row_0'=4,'row_1'=4,'row_2'=2,'col'=8] {'row_0','row_1','row_2'}, dimensions={0} | all-to-all | bytes 2097152 | tf_op jit(solution)/shard_map/all_to_all | solution.py:42
  394.5 13.3 %gather_fusion.1 = bf16[320,64,128]{2,1,0:T(8,128)(2,1)} fusion(bf16[64,64,128]{2,0,1:T(8,128)(2,1)S(1)} %copy.87, s32[1024]{0:T(1024)S(1)} %pad_clamp_fusion), kind=kCustom, calls=%fused_computation.1.clone | custom fusion | bytes 10487040 | tf_op jit(solution)/shard_map/jit(_take)/gather | solution.py:71
  407.8 10.0 %fusion.11 = bf16[64,64,128]{2,0,1:T(8,128)(2,1)S(1)} fusion(bf16[64,5,128,128]{3,2,1,0:T(8,128)(2,1)} %param.16, bf16[64,5,64,128]{3,2,1,0:T(8,128)(2,1)} %bitcast.155, pred[64,5]{1,0:T(8,128)(4,1)S(1)} %copy.67, bf16[64,5]{1,0:T(8,128)(2,1)S(1)} %get-tuple-element.13), kind=kOutput, calls=%fused_computation.28 | convolution fusion | flops 676855808 | bytes 16778176 | tf_op jit(solution)/shard_map/rsab,nrsb->nra/dot_general | solution.py:72
  420.3 92.3 %all-gather.8.cloned.1.call-done = bf16[8,64,8192]{2,1,0:T(8,128)(2,1)} async-done(((bf16[1,64,8192]{2,1,0:T(8,128)(2,1)}), bf16[8,64,8192]{2,1,0:T(8,128)(2,1)}) %all-gather.8.cloned.1.call-update) | async-done | bytes 8388624 | tf_op jit(solution)/shard_map/all_gather | solution.py:15
  518.0 15.8 %psum.137 = f32[64,64]{0,1:T(8,128)S(1)} all-reduce(f32[64,64]{0,1:T(8,128)S(1)} %fusion.47), channel_id=1, replica_groups=mesh['row_0'=4,'row_1'=4,'row_2'=2,'col'=8] {'row_0'}, use_global_device_ids=true, to_apply=%region_19.24 | all-reduce | flops 4096 | bytes 32768 | tf_op jit(solution)/shard_map/psum | solution.py:31
  533.8 17.0 %psum.138 = f32[64,64]{0,1:T(8,128)S(1)} all-reduce(f32[64,64]{0,1:T(8,128)S(1)} %psum.137), channel_id=1, replica_groups=mesh['row_0'=4,'row_1'=4,'row_2'=2,'col'=8] {'row_1'}, use_global_device_ids=true, to_apply=%region_20.25 | all-reduce | flops 4096 | bytes 32768 | tf_op jit(solution)/shard_map/psum | solution.py:31
  554.3 5.8 cholesky.96
  569.7 10.2 %broadcast_multiply_fusion = f32[64,64,5,128]{3,1,2,0:T(8,128)} fusion(f32[64,5]{1,0:T(8,128)S(1)} %get-tuple-element.14, bf16[64,5,128,128]{3,2,1,0:T(8,128)(2,1)} %param.16, bf16[64,64,128,1]{2,1,0,3:T(8,128)(2,1)S(1)} %bitcast.157), kind=kOutput, calls=%fused_computation.13 | convolution fusion | flops 673710080 | bytes 22021376 | tf_op jit(solution)/shard_map/rsab,nra->rsnb/dot_general | solution.py:83
  580.1 33.0 %scatter_fusion.2 = f32[64,64,128]{2,1,0:T(8,128)S(1)} fusion(f32[64,64,128]{2,1,0:T(8,128)S(1)} %broadcast.78, s32[320]{0:T(512)S(1)} %reshape.168, f32[320,64,128]{2,1,0:T(8,128)} %bitcast.152), kind=kCustom, calls=%fused_computation.4 | custom fusion | flops 2621440 | bytes 31458560 | tf_op jit(solution)/shard_map/scatter-add | solution.py:87
  621.8 5.8 cholesky.107
  637.0 15.9 %psum.140 = f32[64,64]{1,0:T(8,128)S(1)} all-reduce(f32[64,64]{1,0:T(8,128)S(1)} %fusion.48), channel_id=1, replica_groups=mesh['row_0'=4,'row_1'=4,'row_2'=2,'col'=8] {'row_0'}, use_global_device_ids=true, to_apply=%region_24.29 | all-reduce | flops 4096 | bytes 32768 | tf_op jit(solution)/shard_map/psum | solution.py:31
  652.9 16.4 %psum.141 = f32[64,64]{1,0:T(8,128)S(1)} all-reduce(f32[64,64]{1,0:T(8,128)S(1)} %psum.140), channel_id=1, replica_groups=mesh['row_0'=4,'row_1'=4,'row_2'=2,'col'=8] {'row_1'}, use_global_device_ids=true, to_apply=%region_25.30 | all-reduce | flops 4096 | bytes 32768 | tf_op jit(solution)/shard_map/psum | solution.py:31
  672.8 28.3 %psum.143 = f32[64,64]{1,0:T(8,128)S(1)} all-reduce(f32[64,64]{1,0:T(8,128)S(1)} %psum.142), channel_id=1, replica_groups=mesh['row_0'=4,'row_1'=4,'row_2'=2,'col'=8] {'col'}, use_global_device_ids=true, to_apply=%region_27.32 | all-reduce | flops 4096 | bytes 32768 | tf_op jit(solution)/shard_map/psum | solution.py:31
  (120 shorter events, 96.8 us)
Async XLA Ops:
  9.1 22.5 %all-to-all-start = ((bf16[32,64,256]{2,1,0:T(8,128)(2,1)}), bf16[32,64,256]{2,1,0:T(8,128)(2,1)S(1)}, u32[]{:S(2)}, u32[]{:S(2)}) async-start(bf16[32,64,256]{2,1,0:T(8,128)(2,1)} %broadcast_in_dim.13), calls=%async_computation | async-start | bytes 2097152 | tf_op jit(solution)/shard_map/all_to_all | solution.py:42
  16.7 44.7 %all-gather.6.cloned.1.call-start = ((), (), s32[]{:S(2)}) async-start(), calls=%async_computation.6 | async-start | bytes 1179648 | tf_op jit(solution)/shard_map/all_gather | solution.py:99
  18.4 137.3 %all-gather.4.cloned.1.call-start = ((), (), s32[]{:S(2)}) async-start(), calls=%async_computation.5 | async-start | bytes 9437184 | tf_op jit(solution)/shard_map/all_gather | solution.py:15
  56.7 2.0 copy-start.6
  130.7 108.5 %copy-start.3 = (bf16[64,8192]{1,0:T(8,128)(2,1)S(1)}, bf16[64,8192]{1,0:T(8,128)(2,1)}, u32[]{:S(2)}) copy-start(bf16[64,8192]{1,0:T(8,128)(2,1)} %all-gather.6.cloned.1.call-done) | copy-start | bytes 3145732
  240.3 1.3 copy-start
  285.7 86.1 %copy-start.4 = (f32[64,256]{1,0:T(8,128)S(1)}, f32[64,256]{1,0:T(8,128)}, u32[]{:S(2)}) copy-start(f32[64,256]{1,0:T(8,128)} %param.15) | copy-start | bytes 196612
  288.4 20.7 %all-to-all-start.2 = ((bf16[32,64,256]{2,1,0:T(8,128)(2,1)}), bf16[32,64,256]{2,1,0:T(8,128)(2,1)S(1)}, u32[]{:S(2)}, u32[]{:S(2)}) async-start(bf16[32,64,256]{2,1,0:T(8,128)(2,1)} %copy.82), calls=%async_computation.2 | async-start | bytes 2097152 | tf_op jit(solution)/shard_map/all_to_all | solution.py:26
  294.2 218.4 %all-gather.8.cloned.1.call-start = ((), (), s32[]{:S(2)}) async-start(), calls=%async_computation.7 | async-start | bytes 9437184 | tf_op jit(solution)/shard_map/all_gather | solution.py:15
  417.9 2.1 copy-start.5
  420.3 146.6 %copy-start.1 = (f32[64,8192]{1,0:T(8,128)S(1)}, f32[64,8192]{1,0:T(8,128)}, u32[]{:S(2)}) copy-start(f32[64,8192]{1,0:T(8,128)} %copy-done) | copy-start | bytes 6291460
  567.9 1.3 copy-start.2
  615.9 20.7 %all-to-all-start.4 = ((bf16[32,64,256]{2,1,0:T(8,128)(2,1)}), bf16[32,64,256]{2,1,0:T(8,128)(2,1)S(1)}, u32[]{:S(2)}, u32[]{:S(2)}) async-start(bf16[32,64,256]{2,1,0:T(8,128)(2,1)} %copy.93), calls=%async_computation.4 | async-start | bytes 2097152 | tf_op jit(solution)/shard_map/all_to_all | solution.py:26
Sparse Core Ops, SparseCore 0:
  19.9 41.4 all-gather.5
  63.2 92.4 all-gather.3
  420.0 92.5 all-gather.7
